TPU v7x, 32 devices: a whole 2x2x4 slice. The times are simulated.
32 devices in a mesh: grp: 4 (over y, x), row: 8 (over z, core).
Axes of the slice: x: 2, y: 2, z: 4, core: 2. Of those that a mesh axis runs over, the one named last changes fastest.
Arguments:
- t_start: bfloat16 [8192, 512], P(('row', 'grp')), may hold values from -6 to 6
- h_blocks: bfloat16 [64, 4, 8, 128, 128], P('row', 'grp'), may hold values from -0.09375 to 0.09375
- h_cols: int32 [64, 4, 8], P('row', 'grp'), may hold values from 0 to 63, as said below
- t_cols: int32 [64, 3], P(('row', 'grp')), may hold values from 0 to 3, as said below
Outputs:
- t_before: bfloat16 [8192, 512], P(('row', 'grp'))
- t_last: bfloat16 [8192, 512], P(('row', 'grp'))
Inputs may be any that keep to these rules, and one draw needn't show every extreme that they name: The 8 entries of h_cols[b, g] differ, and each names a block row c with (c // 2) % 4 == g. `t_cols`: the 3 entries of a row differ.
All inputs are finite; a program needn't handle non-finite values.
Results may differ from a plain program's by a relative error of at most 0.025.
Values may be sent and summed in bfloat16 or wider, within the bound.
A program may use at most 64 MiB of HBM per device.

v0:
```python
import jax
import jax.numpy as jnp
from jax import lax
from jax.sharding import PartitionSpec as P

BS = 128
STEPS = 3


def per_device(t_start, h_blocks, h_cols, t_cols):
    groups = lax.axis_size("grp")
    rows_here = t_start.shape[0] // BS
    width = t_start.shape[1]
    col_blocks = width // BS
    blocks = h_blocks[:, 0]
    columns = h_cols[:, 0]
    local_index = columns // (groups * rows_here) * rows_here + columns % rows_here
    block_ids = jnp.arange(col_blocks, dtype=jnp.int32)
    kept = jnp.any(t_cols[:, :, None] == block_ids[None, None, :], axis=1)
    keep = kept.astype(jnp.float32)[:, None, :, None]

    def masked(values):
        shaped = values.reshape(rows_here, BS, col_blocks, BS) * keep
        return shaped.reshape(rows_here * BS, width)

    def apply_slab(slab):
        gathered = lax.all_gather(slab, "row", axis=0, tiled=True).reshape(-1, BS, width)
        picked = gathered[local_index]
        result = jnp.einsum("rsij,rsjm->rim", blocks, picked, preferred_element_type=jnp.float32)
        summed = lax.psum_scatter(
            result.astype(jnp.bfloat16).astype(jnp.float32).astype(jnp.bfloat16),
            "grp",
            scatter_dimension=0,
            tiled=True,
        ).astype(jnp.float32)
        return summed.reshape(rows_here * BS, width)

    first = masked(apply_slab(t_start)).astype(jnp.bfloat16)
    before, latest = (t_start, first)
    for step in range(STEPS - 1):
        summed = apply_slab(latest)
        after = masked(2.0 * summed - before.astype(jnp.float32)).astype(jnp.bfloat16)
        before, latest = (latest, after)
    return (before, latest)


def solution(mesh):
    placed = (
        P(("row", "grp"), None),
        P("row", "grp", None, None, None),
        P("row", "grp", None),
        P(("row", "grp"), None),
    )
    return jax.shard_map(
        per_device,
        mesh=mesh,
        in_specs=placed,
        out_specs=(P(("row", "grp"), None), P(("row", "grp"), None)),
        check_vma=False,
    )
```

profile of v0, /device:TPU:0, one launch (start us, length us, event | category | flops | bytes accessed | tf_op | source)
XLA Modules:
  0.0 241.6 jit_solution(15152453608066359497)
XLA Ops:
  7.2 0.0 all-gather.4.cloned.1.call-start
  7.2 0.7 all-gather.4.cloned.1.call-update
  7.9 0.0 reduce-scatter.4.cloned.1.call-start
  8.0 0.7 compare_select_fusion
  8.7 0.1 reshape.162
  8.8 32.7 %all-gather.4.cloned.1.call-done = bf16[2048,512]{1,0:T(8,128)(2,1)} async-done(((bf16[256,512]{1,0:T(8,128)(2,1)}), bf16[2048,512]{1,0:T(8,128)(2,1)}) %all-gather.4.cloned.1.call-update) | async-done | bytes 2097168 | tf_op jit(solution)/shard_map/all_gather | solution.py:27
  41.4 7.1 %gather_fusion = bf16[64,128,512]{2,1,0:T(8,128)(2,1)} fusion(bf16[16,128,512]{2,1,0:T(8,128)(2,1)} %bitcast.77, s32[1024]{0:T(1024)S(1)} %pad_clamp_fusion), kind=kCustom, calls=%fused_computation | custom fusion | bytes 16777472 | tf_op jit(solution)/shard_map/gather | solution.py:28
  48.5 7.1 %fusion.12 = bf16[8,128,512]{1,2,0:T(8,128)(2,1)} fusion(bf16[8,8,128,512]{3,2,1,0:T(8,128)(2,1)} %bitcast.81, bf16[8,1,8,128,128]{4,3,2,1,0:T(8,128)(2,1)S(1)} %copy-done), kind=kOutput, calls=%fused_computation.12 | convolution fusion | flops 1074266112 | bytes 11534336 | tf_op jit(solution)/shard_map/rsij,rsjm->rim/dot_general | solution.py:29
  55.7 0.0 reduce-scatter.4.cloned.1.call-update
  55.7 0.0 all-gather.6.cloned.1.call-start
  55.7 0.1 fusion.28
  55.8 27.2 %reduce-scatter.4.cloned.1.call-done = bf16[2,128,512]{1,2,0:T(8,128)(2,1)} async-done(((bf16[8,128,512]{1,2,0:T(8,128)(2,1)}), bf16[2,128,512]{1,2,0:T(8,128)(2,1)}) %reduce-scatter.4.cloned.1.call-update) | async-done | bytes 262160 | tf_op jit(solution)/shard_map/reduce_scatter | solution.py:30
  83.1 1.1 copy.16
  84.1 0.1 mul.56
  84.3 0.8 fusion.21
  85.1 0.0 reduce-scatter.6.cloned.1.call-start
  85.2 29.3 %all-gather.6.cloned.1.call-done = bf16[2048,512]{1,0:T(8,128)(2,1)} async-done(((bf16[256,512]{1,0:T(8,128)(2,1)}), bf16[2048,512]{1,0:T(8,128)(2,1)}) %all-gather.6.cloned.1.call-update) | async-done | bytes 2097168 | tf_op jit(solution)/shard_map/all_gather | solution.py:27
  114.5 7.1 %gather_fusion.1 = bf16[64,128,512]{2,1,0:T(8,128)(2,1)} fusion(bf16[16,128,512]{2,1,0:T(8,128)(2,1)} %bitcast.79, s32[1024]{0:T(1024)S(1)} %pad_clamp_fusion), kind=kCustom, calls=%fused_computation.1 | custom fusion | bytes 16777472 | tf_op jit(solution)/shard_map/gather | solution.py:28
  121.6 7.1 %fusion.15 = bf16[8,128,512]{1,2,0:T(8,128)(2,1)} fusion(bf16[8,8,128,512]{3,2,1,0:T(8,128)(2,1)} %bitcast.82, bf16[8,1,8,128,128]{4,3,2,1,0:T(8,128)(2,1)S(1)} %copy-done), kind=kOutput, calls=%fused_computation.13 | convolution fusion | flops 1074266112 | bytes 11534336 | tf_op jit(solution)/shard_map/rsij,rsjm->rim/dot_general | solution.py:29
  128.7 0.0 all-gather.8.cloned.1.call-start
  128.8 27.4 %reduce-scatter.6.cloned.1.call-done = bf16[2,128,512]{1,2,0:T(8,128)(2,1)} async-done(((bf16[8,128,512]{1,2,0:T(8,128)(2,1)}), bf16[2,128,512]{1,2,0:T(8,128)(2,1)}) %reduce-scatter.6.cloned.1.call-update) | async-done | bytes 262160 | tf_op jit(solution)/shard_map/reduce_scatter | solution.py:30
  156.1 1.8 convert_multiply_fusion.1
  157.9 1.2 copy.18
  159.2 0.8 fusion.22
  160.0 0.2 reduce-scatter.8.cloned.1.call-start
  160.3 29.0 %all-gather.8.cloned.1.call-done = bf16[2048,512]{1,0:T(8,128)(2,1)} async-done(((bf16[256,512]{1,0:T(8,128)(2,1)}), bf16[2048,512]{1,0:T(8,128)(2,1)}) %all-gather.8.cloned.1.call-update) | async-done | bytes 2097168 | tf_op jit(solution)/shard_map/all_gather | solution.py:27
  189.3 7.1 %gather_fusion.2 = bf16[64,128,512]{2,1,0:T(8,128)(2,1)} fusion(bf16[16,128,512]{2,1,0:T(8,128)(2,1)} %bitcast.78, s32[1024]{0:T(1024)S(1)} %pad_clamp_fusion), kind=kCustom, calls=%fused_computation.2 | custom fusion | bytes 16777472 | tf_op jit(solution)/shard_map/gather | solution.py:28
  196.3 7.1 %fusion.18 = bf16[8,128,512]{1,2,0:T(8,128)(2,1)} fusion(bf16[8,8,128,512]{3,2,1,0:T(8,128)(2,1)} %bitcast.80, bf16[8,1,8,128,128]{4,3,2,1,0:T(8,128)(2,1)S(1)} %copy-done), kind=kOutput, calls=%fused_computation.14 | convolution fusion | flops 1074266112 | bytes 11534336 | tf_op jit(solution)/shard_map/rsij,rsjm->rim/dot_general | solution.py:29
  203.5 27.4 %reduce-scatter.8.cloned.1.call-done = bf16[2,128,512]{1,2,0:T(8,128)(2,1)} async-done(((bf16[8,128,512]{1,2,0:T(8,128)(2,1)}), bf16[2,128,512]{1,2,0:T(8,128)(2,1)}) %reduce-scatter.8.cloned.1.call-update) | async-done | bytes 262160 | tf_op jit(solution)/shard_map/reduce_scatter | solution.py:30
  230.9 1.8 convert_multiply_fusion
  232.7 1.2 copy.20
  233.9 0.8 fusion.23
  (14 shorter events, 0.1 us)
Async XLA Ops:
  7.2 41.4 %copy-start = (bf16[8,1,8,128,128]{4,3,2,1,0:T(8,128)(2,1)S(1)}, bf16[8,1,8,128,128]{4,3,2,1,0:T(8,128)(2,1)}, u32[]{:S(2)}) copy-start(bf16[8,1,8,128,128]{4,3,2,1,0:T(8,128)(2,1)} %param.5) | copy-start | bytes 6291460
  7.2 34.3 %all-gather.4.cloned.1.call-start = ((), (), s32[]{:S(2)}) async-start(), calls=%async_computation.3 | async-start | bytes 2359296 | tf_op jit(solution)/shard_map/all_gather | solution.py:27
  7.9 75.1 %reduce-scatter.4.cloned.1.call-start = ((), (), s32[]{:S(2)}) async-start(), calls=%async_computation.4 | async-start | bytes 1310720 | tf_op jit(solution)/shard_map/reduce_scatter | solution.py:30
  48.5 7.2 %copy-start.3 = (s32[2,3]{1,0:T(2,128)S(1)}, s32[2,3]{1,0:T(2,128)}, u32[]{:S(2)}) copy-start(s32[2,3]{1,0:T(2,128)} %param.7) | copy-start | bytes 76
  55.7 58.8 %all-gather.6.cloned.1.call-start = ((), (), s32[]{:S(2)}) async-start(), calls=%async_computation.5 | async-start | bytes 2359296 | tf_op jit(solution)/shard_map/all_gather | solution.py:27
  85.1 71.0 %reduce-scatter.6.cloned.1.call-start = ((), (), s32[]{:S(2)}) async-start(), calls=%async_computation.6 | async-start | bytes 1310720 | tf_op jit(solution)/shard_map/reduce_scatter | solution.py:30
  121.6 37.6 %copy-start.2 = (bf16[256,512]{1,0:T(8,128)(2,1)S(1)}, bf16[256,512]{1,0:T(8,128)(2,1)}, u32[]{:S(2)}) copy-start(bf16[256,512]{1,0:T(8,128)(2,1)} %param.4) | copy-start | bytes 786436
  128.7 60.5 %all-gather.8.cloned.1.call-start = ((), (), s32[]{:S(2)}) async-start(), calls=%async_computation.7 | async-start | bytes 2359296 | tf_op jit(solution)/shard_map/all_gather | solution.py:27
  160.0 70.9 %reduce-scatter.8.cloned.1.call-start = ((), (), s32[]{:S(2)}) async-start(), calls=%async_computation.8 | async-start | bytes 1310720 | tf_op jit(solution)/shard_map/reduce_scatter | solution.py:30
  196.3 37.6 %copy-start.1 = (bf16[256,512]{1,0:T(8,128)(2,1)S(1)}, bf16[256,512]{1,0:T(8,128)(2,1)}, u32[]{:S(2)}) copy-start(bf16[256,512]{1,0:T(8,128)(2,1)} %fusion.21) | copy-start | bytes 786436
Sparse Core Ops, SparseCore 0:
  9.6 31.7 all-gather.3
  55.8 27.2 reduce-scatter.3
  85.3 29.1 all-gather.5
  128.8 27.2 reduce-scatter.5
  160.1 29.0 all-gather.7
  203.6 27.2 reduce-scatter.7
where the time goes:
time: 242 us
  waiting for transfers between devices  174 us (72%)
  local copies, waits for them, and re-layouts  25 us (10%)
  matrix products  21.4 us (9%)
  between operations  14.2 us (6%)
  other arithmetic  6.82 us (3%)
    all_gather x3, waiting for transfers between devices, apply_slab(): lax.all_gather(slab, 'row', axis=0, tiled=True).reshape(-1, BS, width)  91 us
    reduce_scatter x3, waiting for transfers between devices, apply_slab(): lax.psum_scatter(result.astype(jnp.bfloat16).astype(jnp.float32).astype(j...  82 us
    dot_general x3, matrix products, apply_slab(): jnp.einsum('rsij,rsjm->rim', blocks, picked, preferred_element_type=jnp.f...  21.4 us
    gather x3, local copies, waits for them, and re-layouts, apply_slab(): picked = gathered[local_index]  21.3 us
  transfers between devices with their start and end apart: 6, of which 6 were waited for; matrix products, arithmetic and copies ran while one was open for 0% of the time, Pallas kernels for 0%

commit v1 on v0

v1 whole, which is shorter than its diff:
```python
import functools

import jax
import jax.numpy as jnp
from jax import lax
from jax.experimental import pallas as pl
from jax.experimental.pallas import tpu as pltpu
from jax.sharding import PartitionSpec as P

BS = 128
STEPS = 3
MESH = pl.DeviceIdType.MESH
BF16 = jnp.bfloat16
F32 = jnp.float32
DENSE_BYTES = 8 << 20


def kernel(dims, t_hbm, h_hbm, hc, tc, before_ref, last_ref, *scratch):
    groups, rows, rb, cb, keeps, hrows, slots, dense = dims
    bufs = scratch[:STEPS]
    hs, hd, unp, prod, stage, landed, drow, dgrp = scratch[STEPS : STEPS + 8]
    ag_s, ag_r, fw_s, fw_r, rs_s, rs_r, dr_s, dr_r, dg_s, dg_r, local = scratch[STEPS + 8 :]
    pairs = rows // 2
    nblk = rows * rb
    g = lax.axis_index("grp")
    r = lax.axis_index("row")
    pair, core = r // 2, lax.rem(r, 2)
    sibling = pair * 2 + 1 - core
    mine = pl.ds(r * rb, rb)

    def copy(src, dst, ss, rs, row=None, grp=None):
        return pltpu.make_async_remote_copy(
            src_ref=src,
            dst_ref=dst,
            send_sem=ss,
            recv_sem=rs,
            device_id=(g if grp is None else grp, r if row is None else row),
            device_id_type=MESH,
        )

    h_copy = pltpu.make_async_copy(h_hbm.at[:, 0], hs.at[:, pl.ds(0, slots)], local.at[cb])
    h_copy.start()
    barrier = pltpu.get_barrier_semaphore()
    for k in range(1, rows):
        pl.semaphore_signal(barrier, inc=1, device_id=(g, lax.rem(r + k, rows)), device_id_type=MESH)
    for k in range(1, groups):
        pl.semaphore_signal(barrier, inc=1, device_id=(lax.rem(g + k, groups), r), device_id_type=MESH)

    t_copies = []
    for c in range(cb):
        for b in range(rb):
            one = pltpu.make_async_copy(
                t_hbm.at[pl.ds(b * BS, BS), pl.ds(c * BS, BS)],
                bufs[0].at[c, r * rb + b],
                local.at[cb + 1 + c * rb + b],
            )
            one.start()
            t_copies.append(one)
    for b in range(rb):
        total = tc[b, 0]
        for s in range(1, keeps):
            total = total + tc[b, s]
        gone = cb * (cb - 1) // 2 - total
        tile = jnp.full((16, BS), gone, jnp.int32).astype(F32).astype(BF16)
        drow[r, b] = tile
        dgrp[g, b] = tile
    for one in t_copies:
        one.wait()
    pl.semaphore_wait(barrier, rows + groups - 2)

    sends = []

    def go(one):
        one.start()
        sends.append(one)

    def gather_start(chunk, buf, c):
        own = buf.at[c, mine]
        for k in range(1, pairs):
            go(copy(own, own, ag_s.at[chunk, k], ag_r.at[chunk, k], row=lax.rem(pair + k, pairs) * 2 + core))
        go(copy(own, own, fw_s.at[chunk, 0], fw_r.at[chunk, 0], row=sibling))

    def gather_finish(chunk, buf, c):
        for k in range(1, pairs):
            src = lax.rem(pair + pairs - k, pairs)
            got = buf.at[c, pl.ds((src * 2 + core) * rb, rb)]
            copy(got, got, ag_s.at[chunk, k], ag_r.at[chunk, k], row=sibling).wait_recv()
            go(copy(got, got, fw_s.at[chunk, k], fw_r.at[chunk, k], row=sibling))
        for k in range(pairs):
            src = lax.rem(pair + pairs - k, pairs)
            got = buf.at[c, pl.ds((src * 2 + 1 - core) * rb, rb)]
            copy(got, got, fw_s.at[chunk, k], fw_r.at[chunk, k], row=sibling).wait_recv()

    for k in range(1, rows):
        go(copy(drow.at[r], drow.at[r], dr_s.at[k], dr_r.at[k], row=lax.rem(r + k, rows)))
    for k in range(1, groups):
        go(copy(dgrp.at[g], dgrp.at[g], dg_s.at[k], dg_r.at[k], grp=lax.rem(g + k, groups)))
    for c in range(cb):
        gather_start(c, bufs[0], c)

    hs[:, slots] = jnp.zeros((hrows, BS, BS), BF16)
    h_copy.wait()
    if dense:

        def build(b, carry):
            for c in range(nblk):
                named = (c // rb) * (groups * rb) + g * rb + c % rb
                at = jnp.int32(slots)
                for s in range(slots):
                    at = jnp.where(hc[b, 0, s] == named, s, at)
                hd[pl.ds(pl.multiple_of(b * BS, BS), BS), c * BS : (c + 1) * BS] = hs[b, at]
            return carry

        lax.fori_loop(0, hrows, build, 0)

    for k in range(1, rows):
        got = drow.at[lax.rem(r + rows - k, rows)]
        copy(got, got, dr_s.at[k], dr_r.at[k], row=sibling).wait_recv()
    for k in range(1, groups):
        got = dgrp.at[lax.rem(g + groups - k, groups)]
        copy(got, got, dg_s.at[k], dg_r.at[k], row=sibling).wait_recv()

    def full(tile):
        return jnp.concatenate([tile] * (BS // 16), axis=0)

    def unpacked(c, gone, packed):
        zero = jnp.zeros((BS, BS), BF16)
        if c == 0:
            value = packed(0)
        elif c == cb - 1:
            value = packed(c - 1)
        else:
            value = jnp.where(gone < c, packed(c - 1), packed(c))
        return jnp.where(gone == c, zero, value)

    def multiply(c, x):
        if dense:
            right = x[...].reshape(nblk * BS, BS)
            out = jnp.dot(hd[...], right, preferred_element_type=F32)
            prod[c] = out.astype(BF16).reshape(hrows, BS, BS)
            return

        def one_row(b, carry):
            out = jnp.zeros((BS, BS), F32)
            for s in range(slots):
                named = hc[b, 0, s]
                at = named // (groups * rb) * rb + lax.rem(named, rb)
                out = out + jnp.dot(hs[b, s], x[at], preferred_element_type=F32)
            prod[c, b] = out.astype(BF16)
            return carry

        lax.fori_loop(0, hrows, one_row, 0)

    def unpack_column(c, buf):
        def one(j, carry):
            gone = full(drow[j // rb, lax.rem(j, rb)])
            unp[c, j] = unpacked(c, gone, lambda p: buf[p, j])
            return carry

        lax.fori_loop(0, nblk, one, 0)

    def scatter_start(step, p):
        def one(i, carry):
            gone = full(dgrp[i // rb, lax.rem(i, rb)])
            stage[step, p, i] = jnp.where(gone > p, prod[p, i], prod[p + 1, i])
            return carry

        lax.fori_loop(0, hrows, one, 0)
        for k in range(1, groups):
            to = lax.rem(g + k, groups)
            go(copy(
                stage.at[step, p, pl.ds(to * rb, rb)],
                landed.at[step, p, g],
                rs_s.at[step * keeps + p, k],
                rs_r.at[step * keeps + p, k],
                grp=to,
            ))

    def scatter_finish(step, p):
        for k in range(1, groups):
            got = landed.at[step, p, lax.rem(g + groups - k, groups)]
            copy(got, got, rs_s.at[step * keeps + p, k], rs_r.at[step * keeps + p, k], row=sibling).wait_recv()
        for b in range(rb):
            gone = full(drow[r, b])
            total = stage[step, p, g * rb + b].astype(F32)
            for k in range(1, groups):
                total = total + landed[step, p, lax.rem(g + k, groups), b].astype(F32)
            at = r * rb + b
            if step == 0:
                new = total
            else:
                if step == 1:
                    old = jnp.where(gone > p, bufs[0][p, at], bufs[0][p + 1, at])
                else:
                    old = bufs[step - 1][p, at]
                new = 2.0 * total - old.astype(F32)
            new = new.astype(BF16)
            if step < STEPS - 1:
                bufs[step + 1][p, at] = new
            else:
                stage[step, p, g * rb + b] = new
        if step < STEPS - 1:
            gather_start(cb + step * keeps + p, bufs[step + 1], p)

    for step in range(STEPS):
        buf = bufs[step]
        for c in range(cb):
            if step == 0:
                gather_finish(c, buf, c)
                multiply(c, buf.at[c])
            else:
                if c < keeps:
                    gather_finish(cb + (step - 1) * keeps + c, buf, c)
                unpack_column(c, buf)
                multiply(c, unp.at[c])
            if c >= 1:
                scatter_start(step, c - 1)
            if c >= 2:
                scatter_finish(step, c - 2)
        scatter_finish(step, keeps - 1)

    for b in range(rb):
        gone = full(drow[r, b])
        for c in range(cb):
            here = (slice(b * BS, (b + 1) * BS), slice(c * BS, (c + 1) * BS))
            before_ref[here] = unpacked(c, gone, lambda p: bufs[STEPS - 1][p, r * rb + b])
            last_ref[here] = unpacked(c, gone, lambda p: stage[STEPS - 1, p, g * rb + b])
    for one in sends:
        one.wait_send()


def per_device(t_start, h_blocks, h_cols, t_cols):
    groups, rows = lax.axis_size("grp"), lax.axis_size("row")
    rb, cb = t_start.shape[0] // BS, t_start.shape[1] // BS
    hrows, slots = h_blocks.shape[0], h_blocks.shape[2]
    keeps = t_cols.shape[1]
    nblk = rows * rb
    pairs = rows // 2
    dense = hrows * nblk * BS * BS * 2 <= DENSE_BYTES
    chunks = cb + (STEPS - 1) * keeps
    dma = pltpu.SemaphoreType.DMA
    out = jax.ShapeDtypeStruct(t_start.shape, t_start.dtype)
    return pl.pallas_call(
        functools.partial(kernel, (groups, rows, rb, cb, keeps, hrows, slots, dense)),
        out_shape=(out, out),
        in_specs=[
            pl.BlockSpec(memory_space=pl.ANY),
            pl.BlockSpec(memory_space=pl.ANY),
            pl.BlockSpec(memory_space=pltpu.SMEM),
            pl.BlockSpec(memory_space=pltpu.SMEM),
        ],
        out_specs=(pl.BlockSpec(memory_space=pltpu.VMEM),) * 2,
        scratch_shapes=[
            pltpu.VMEM((cb, nblk, BS, BS), BF16),
            *[pltpu.VMEM((keeps, nblk, BS, BS), BF16) for _ in range(STEPS - 1)],
            pltpu.VMEM((hrows, slots + 1, BS, BS), BF16),
            pltpu.VMEM((hrows * BS, nblk * BS) if dense else (16, BS), BF16),
            pltpu.VMEM((cb, nblk, BS, BS), BF16),
            pltpu.VMEM((cb, hrows, BS, BS), BF16),
            pltpu.VMEM((STEPS, keeps, hrows, BS, BS), BF16),
            pltpu.VMEM((STEPS, keeps, groups, rb, BS, BS), BF16),
            pltpu.VMEM((rows, rb, 16, BS), BF16),
            pltpu.VMEM((groups, rb, 16, BS), BF16),
            dma((chunks, pairs)),
            dma((chunks, pairs)),
            dma((chunks, pairs)),
            dma((chunks, pairs)),
            dma((STEPS * keeps, groups)),
            dma((STEPS * keeps, groups)),
            dma((rows,)),
            dma((rows,)),
            dma((groups,)),
            dma((groups,)),
            dma((cb + 1 + cb * rb,)),
        ],
        compiler_params=pltpu.CompilerParams(
            collective_id=0, has_side_effects=True, vmem_limit_bytes=56 << 20
        ),
    )(t_start, h_blocks, h_cols, t_cols)


def solution(mesh):
    placed = (
        P(("row", "grp"), None),
        P("row", "grp", None, None, None),
        P("row", "grp", None),
        P(("row", "grp"), None),
    )
    return jax.shard_map(
        per_device,
        mesh=mesh,
        in_specs=placed,
        out_specs=(P(("row", "grp"), None), P(("row", "grp"), None)),
        check_vma=False,
    )
```

time: 242 us -> 96.1 us (0.40)
  waiting for transfers between devices: 174 us -> 0 us
  Pallas kernels: 0 us -> 91 us
  local copies, waits for them, and re-layouts: 25 us -> 3.34 us
  matrix products: 21.4 us -> 0 us
  between operations: 14.2 us -> 0.64 us
  other arithmetic: 6.82 us -> 0 us
    all_gather x3 -> x0, waiting for transfers between devices: 91 us -> none  [apply_slab(): lax.all_gather(slab, 'row', axis=0, tiled=True).reshape(-1, BS, width)]
    pallas_call x0 -> x1, Pallas kernels: none -> 91 us  [per_device(): pl.pallas_call(functools.partial(kernel, (groups, rows, rb, cb, keeps, hr...]
    reduce_scatter x3 -> x0, waiting for transfers between devices: 82 us -> none  [apply_slab(): lax.psum_scatter(result.astype(jnp.bfloat16).astype(jnp.float32).astype(j...]
    dot_general x3 -> x0, matrix products: 21.4 us -> none  [apply_slab(): jnp.einsum('rsij,rsjm->rim', blocks, picked, preferred_element_type=jnp.f...]
    gather x3 -> x0, local copies, waits for them, and re-layouts: 21.3 us -> none  [apply_slab(): picked = gathered[local_index]]
    mul x2 -> x0, other arithmetic: 3.56 us -> none  [per_device(): 2.0 * summed - before.astype(jnp.float32)]
    unnamed x8 -> x2, local copies, waits for them, and re-layouts: 0.02 us -> 3.34 us
    mul x3 -> x0, local copies, waits for them, and re-layouts: 2.61 us -> none  [the longest x2 2.47 us: per_device(): 2.0 * summed - before.astype(jnp.float32)]
  transfers between devices with their start and end apart: 6 -> 0, of which waited for: 6 -> 0; matrix products, arithmetic and copies ran while one was open for 0% -> 0% of each run, Pallas kernels for 0% -> 0%
where the time goes in v1:
time: 96.1 us; the launch traced here: 95 us
  Pallas kernels  91 us (95%)
  local copies, waits for them, and re-layouts  3.34 us (3%)
    pallas_call x1, Pallas kernels, per_device(): pl.pallas_call(functools.partial(kernel, (groups, rows, rb, cb, keeps, hr...  91 us
    unnamed x2, local copies, waits for them, and re-layouts  3.34 us

profile of v1, /device:TPU:0, one launch (start us, length us, event | category | flops | bytes accessed | tf_op | source)
XLA Modules:
  0.0 95.0 jit_solution(6185944844942097675)
XLA Ops:
  0.6 91.0 %shard_map.59 = (bf16[256,512]{1,0:T(8,128)(2,1)}, bf16[256,512]{1,0:T(8,128)(2,1)}) custom-call(bf16[256,512]{1,0:T(8,128)(2,1)} %t_hbm.1, bf16[8,1,8,128,128]{4,3,2,1,0:T(8,128)(2,1)} %h_hbm.1, s32[8,1,8]{2,1,0:T(1,128)} %hc.1, s32[2,3]{1,0:T(2,128)} %tc.1), custom_call_target="tpu_custom_call" | custom-call | tf_op jit(solution)/shard_map/pallas_call | solution.py:243
  91.6 1.7 %copy.8 = bf16[256,512]{1,0:T(8,128)(2,1)} copy(bf16[256,512]{1,0:T(8,128)(2,1)} %get-tuple-element.4) | data formatting | bytes 524288
  93.3 1.7 %copy.9 = bf16[256,512]{1,0:T(8,128)(2,1)} copy(bf16[256,512]{1,0:T(8,128)(2,1)} %get-tuple-element.5) | data formatting | bytes 524288

commit v2 on v1

--- a/solution.py
+++ b/solution.py
@@ -95,7 +95,7 @@
         go(copy(drow.at[r], drow.at[r], dr_s.at[k], dr_r.at[k], row=lax.rem(r + k, rows)))
     for k in range(1, groups):
         go(copy(dgrp.at[g], dgrp.at[g], dg_s.at[k], dg_r.at[k], grp=lax.rem(g + k, groups)))
-    for c in range(cb):
+    for c in range(2):
         gather_start(c, bufs[0], c)
 
     hs[:, slots] = jnp.zeros((hrows, BS, BS), BF16)
@@ -112,13 +112,6 @@
             return carry
 
         lax.fori_loop(0, hrows, build, 0)
-
-    for k in range(1, rows):
-        got = drow.at[lax.rem(r + rows - k, rows)]
-        copy(got, got, dr_s.at[k], dr_r.at[k], row=sibling).wait_recv()
-    for k in range(1, groups):
-        got = dgrp.at[lax.rem(g + groups - k, groups)]
-        copy(got, got, dg_s.at[k], dg_r.at[k], row=sibling).wait_recv()
 
     def full(tile):
         return jnp.concatenate([tile] * (BS // 16), axis=0)
@@ -207,12 +200,21 @@
         for c in range(cb):
             if step == 0:
                 gather_finish(c, buf, c)
+                if c + 2 < cb:
+                    gather_start(c + 2, buf, c + 2)
                 multiply(c, buf.at[c])
             else:
                 if c < keeps:
                     gather_finish(cb + (step - 1) * keeps + c, buf, c)
                 unpack_column(c, buf)
                 multiply(c, unp.at[c])
+            if step == 0 and c == 1:
+                for k in range(1, rows):
+                    got = drow.at[lax.rem(r + rows - k, rows)]
+                    copy(got, got, dr_s.at[k], dr_r.at[k], row=sibling).wait_recv()
+                for k in range(1, groups):
+                    got = dgrp.at[lax.rem(g + groups - k, groups)]
+                    copy(got, got, dg_s.at[k], dg_r.at[k], row=sibling).wait_recv()
             if c >= 1:
                 scatter_start(step, c - 1)
             if c >= 2:

time: 96.1 us -> 92.2 us (0.959)
  Pallas kernels: 91 us -> 87.9 us
    pallas_call x1, Pallas kernels: 91 us -> 87.9 us  [per_device(): pl.pallas_call(functools.partial(kernel, (groups, rows, rb, cb, keeps, hr...]
where the time goes in v2:
time: 92.2 us; the launch traced here: 91.9 us
  Pallas kernels  87.9 us (95%)
  local copies, waits for them, and re-layouts  3.34 us (4%)
    pallas_call x1, Pallas kernels, per_device(): pl.pallas_call(functools.partial(kernel, (groups, rows, rb, cb, keeps, hr...  87.9 us
    unnamed x2, local copies, waits for them, and re-layouts  3.34 us

profile of v2, /device:TPU:0, one launch (start us, length us, event | category | flops | bytes accessed | tf_op | source)
XLA Modules:
  0.0 91.9 jit_solution(15069783629652526109)
XLA Ops:
  0.6 87.9 %shard_map.59 = (bf16[256,512]{1,0:T(8,128)(2,1)}, bf16[256,512]{1,0:T(8,128)(2,1)}) custom-call(bf16[256,512]{1,0:T(8,128)(2,1)} %t_hbm.1, bf16[8,1,8,128,128]{4,3,2,1,0:T(8,128)(2,1)} %h_hbm.1, s32[8,1,8]{2,1,0:T(1,128)} %hc.1, s32[2,3]{1,0:T(2,128)} %tc.1), custom_call_target="tpu_custom_call" | custom-call | tf_op jit(solution)/shard_map/pallas_call | solution.py:245
  88.6 1.7 %copy.8 = bf16[256,512]{1,0:T(8,128)(2,1)} copy(bf16[256,512]{1,0:T(8,128)(2,1)} %get-tuple-element.4) | data formatting | bytes 524288
  90.3 1.7 %copy.9 = bf16[256,512]{1,0:T(8,128)(2,1)} copy(bf16[256,512]{1,0:T(8,128)(2,1)} %get-tuple-element.5) | data formatting | bytes 524288
